TPU v7x, 32 devices: a whole 2x2x4 slice. The times are simulated.
32 devices in a mesh: grp: 2 (over y), aux: 8 (over z, x), vec: 2 (over core).
Axes of the slice: x: 2, y: 2, z: 4, core: 2. Of those that a mesh axis runs over, the one named last changes fastest.
Arguments:
- trial: bfloat16 [8, 4736, 640], P(('grp', 'vec'), 'aux'), parts along dimension 0, may hold values from -6 to 6
- b_occ: bfloat16 [12, 640, 640], P('grp'), parts along dimension 0, may hold values from -0.0625 to 0.0625
- b_vir: bfloat16 [12, 4736, 4736], P('grp', 'aux'), parts along dimension 0, may hold values from -0.0625 to 0.0625
- b_mixed: bfloat16 [12, 4736, 640], P('grp', 'aux'), parts along dimension 0, may hold values from -0.0625 to 0.0625
- e_occ: float32 [1280], P('grp'), parts along dimension 0, may hold values from -1 to -0.3
- e_vir: float32 [9472], P(('grp', 'aux')), parts along dimension 0, may hold values from 0.05 to 1.5
- active: int32 [4], P('grp'), parts along dimension 0, may hold values from 0 to 3, as said below
Outputs:
- sigma: bfloat16 [8, 4736, 640], P(('grp', 'vec'), 'aux'), parts along dimension 0
There are 2 independent parts, one for each index of `grp`. A program takes and returns all parts, laid end to end along the dimension named above; each array names one. Nothing has to cross between parts.
Inputs may be any that keep to these rules, and one draw needn't show every extreme that they name: `active`: 2 distinct trial-vector ids in increasing order; the last trial vector, 3, is always among them.
All inputs are finite; a program needn't handle non-finite values.
Results may differ from a plain program's by a relative error of at most 0.0023.
Values may be sent and summed in bfloat16 or wider, within the bound.
A program may use at most 128 MiB of HBM per device.

v0:
```python
import jax
import jax.numpy as jnp
from jax import lax
from jax.sharding import PartitionSpec as P


def fitted_total(partial_value):
    return lax.psum(partial_value, "aux")


def products(chosen, b_occ, b_vir, b_mixed, e_occ, e_vir):
    partial_value = jnp.einsum("paj,vaj->vp", b_mixed, chosen, preferred_element_type=jnp.float32)
    every_row = lax.all_gather(chosen, "aux", axis=1, tiled=True)
    inner = jnp.einsum("pab,vbj->vpaj", b_vir, every_row, preferred_element_type=jnp.float32)
    fit = fitted_total(partial_value)
    exch = jnp.einsum(
        "vpaj,pij->vai", inner.astype(jnp.bfloat16), b_occ, preferred_element_type=jnp.float32
    )
    coul = jnp.einsum(
        "vp,paj->vaj", fit, b_mixed.astype(jnp.float32), precision=lax.Precision.HIGHEST
    )
    gaps = e_vir[:, None] - e_occ[None, :]
    return gaps[None] * chosen.astype(jnp.float32) + 2.0 * coul - exch


def local(trial, b_occ, b_vir, b_mixed, e_occ, e_vir, active):
    local_count = trial.shape[0]
    owned = lax.axis_index("vec") * local_count + jnp.arange(local_count, dtype=jnp.int32)
    values = products(trial, b_occ, b_vir, b_mixed, e_occ, e_vir)
    keeper = jnp.any(owned[:, None] == active[None, :], axis=1).astype(jnp.float32)
    return (values * keeper[:, None, None]).astype(jnp.bfloat16)


def solution(mesh):
    in_specs = (
        P(("grp", "vec"), "aux", None),
        P("grp", None, None),
        P("grp", "aux", None),
        P("grp", "aux", None),
        P("grp"),
        P(("grp", "aux")),
        P("grp"),
    )
    out_specs = P(("grp", "vec"), "aux", None)
    return jax.shard_map(local, mesh=mesh, in_specs=in_specs, out_specs=out_specs, check_vma=False)
```

profile of v0, /device:TPU:0, one launch (start us, length us, event | category | flops | bytes accessed | tf_op | source)
XLA Modules:
  0.0 256.1 jit_solution(129778789523734303)
XLA Ops:
  6.5 0.0 all-gather.2.cloned.1.call-start
  6.5 0.7 all-gather.2.cloned.1.call-update
  7.3 0.0 copy-start.4
  7.3 0.0 copy-start.2
  7.3 0.0 copy-start.3
  7.3 7.3 %fusion.19 = f32[2,6]{1,0:T(2,128)S(1)} fusion(bf16[6,592,640]{2,1,0:T(8,128)(2,1)} %param.10, bf16[2,592,640]{2,1,0:T(8,128)(2,1)} %param.7), kind=kOutput, calls=%fused_computation.17 | convolution fusion | flops 9093120 | bytes 6062128 | tf_op jit(solution)/shard_map/paj,vaj->vp/dot_general | solution.py:12
  14.6 23.7 %psum.7 = f32[2,6]{1,0:T(2,128)S(1)} all-reduce(f32[2,6]{1,0:T(2,128)S(1)} %fusion.19), channel_id=1, replica_groups=mesh['grp'=2,'aux'=8,'vec'=2] {'aux'}, use_global_device_ids=true, to_apply=%region_0.0 | all-reduce | flops 12 | bytes 96 | tf_op jit(solution)/shard_map/psum | solution.py:8
  38.4 0.0 copy-done.4
  38.4 0.2 compare_reduce_fusion
  38.6 0.0 copy-done.2
  38.6 0.0 copy-done.3
  38.6 1.3 broadcast_subtract_fusion
  39.9 7.2 %fusion.6 = f32[2,592,640]{2,0,1:T(2,128)S(1)} fusion(bf16[6,592,640]{2,1,0:T(8,128)(2,1)} %param.10, f32[2,6]{1,0:T(2,128)S(1)} %psum.7), kind=kOutput, calls=%fused_computation.6 | convolution fusion | flops 54558720 | bytes 7577648 | tf_op jit(solution)/shard_map/vp,paj->vaj/dot_general | solution.py:19
  47.0 136.4 %all-gather.2.cloned.1.call-done = bf16[2,4736,640]{2,1,0:T(8,128)(2,1)} async-done(((bf16[2,592,640]{2,1,0:T(8,128)(2,1)}), bf16[2,4736,640]{2,1,0:T(8,128)(2,1)}) %all-gather.2.cloned.1.call-update) | async-done | bytes 12124176 | tf_op jit(solution)/shard_map/all_gather | solution.py:13
  183.5 0.0 copy-start
  183.5 0.0 copy-start.1
  183.5 53.5 %fusion = bf16[2,640,6,592]{1,3,2,0:T(8,128)(2,1)} fusion(bf16[6,592,4736]{2,1,0:T(8,128)(2,1)} %param.9, bf16[2,4736,640]{2,1,0:T(8,128)(2,1)} %all-gather.2.cloned.1.call-done), kind=kOutput, calls=%fused_computation | convolution fusion | flops 43065016320 | bytes 54861824 | tf_op jit(solution)/shard_map/pab,vbj->vpaj/dot_general | solution.py:14
  237.0 0.0 copy-done
  237.0 0.0 copy-done.1
  237.0 12.2 %fusion.12 = bf16[2,592,640]{2,1,0:T(8,128)(2,1)} fusion(f32[2,592,640]{2,0,1:T(2,128)S(1)} %fusion.6, bf16[2,592,640]{2,1,0:T(8,128)(2,1)S(1)} %copy-done, bf16[6,640,640]{2,1,0:T(8,128)(2,1)} %param.8, bf16[2,640,6,592]{1,3,2,0:T(8,128)(2,1)} %fusion, f32[2]{0:T(128)S(1)} %convert_element_type.23, f32[592,640]{1,0:T(8,128)S(1)} %copy-done.1), kind=kOutput, calls=%fused_computation.13 | convolution fusion | flops 5824901120 | bytes 21585928 | tf_op jit(solution)/shard_map/vpaj,pij->vai/dot_general | solution.py:16
  (2 shorter events, 0.0 us)
Async XLA Ops:
  6.5 176.9 %all-gather.2.cloned.1.call-start = ((), (), s32[]{:S(2)}) async-start(), calls=%async_computation | async-start | bytes 13639680 | tf_op jit(solution)/shard_map/all_gather | solution.py:13
  7.3 31.1 %copy-start.4 = (s32[2]{0:T(128)S(1)}, s32[2]{0:T(128)}, u32[]{:S(2)}) copy-start(s32[2]{0:T(128)} %param.13) | copy-start | bytes 28
  7.3 31.3 %copy-start.2 = (f32[640]{0:T(1024)S(1)}, f32[640]{0:T(1024)}, u32[]{:S(2)}) copy-start(f32[640]{0:T(1024)} %param.11) | copy-start | bytes 7684
  7.3 31.3 %copy-start.3 = (f32[592]{0:T(1024)S(1)}, f32[592]{0:T(1024)}, u32[]{:S(2)}) copy-start(f32[592]{0:T(1024)} %param.12) | copy-start | bytes 7108
  183.5 53.5 %copy-start = (bf16[2,592,640]{2,1,0:T(8,128)(2,1)S(1)}, bf16[2,592,640]{2,1,0:T(8,128)(2,1)}, u32[]{:S(2)}) copy-start(bf16[2,592,640]{2,1,0:T(8,128)(2,1)} %param.7) | copy-start | bytes 4546564
  183.5 53.5 %copy-start.1 = (f32[592,640]{1,0:T(8,128)S(1)}, f32[592,640]{1,0:T(8,128)}, u32[]{:S(2)}) copy-start(f32[592,640]{1,0:T(8,128)} %broadcast_subtract_fusion) | copy-start | bytes 4546564
Sparse Core Ops, SparseCore 0:
  9.6 173.8 all-gather.1
where the time goes:
time: 256 us
  waiting for transfers between devices  137 us (54%)
  matrix products  80.2 us (31%)
  blocking collectives  23.7 us (9%)
  between operations  13.4 us (5%)
    all_gather x1, waiting for transfers between devices, products(): every_row = lax.all_gather(chosen, 'aux', axis=1, tiled=True)  136 us
    dot_general x1, matrix products, products(): jnp.einsum('pab,vbj->vpaj', b_vir, every_row, preferred_element_type=jnp....  53.5 us
    psum x1, blocking collectives, fitted_total(): return lax.psum(partial_value, 'aux')  23.7 us
    dot_general x1, matrix products, products(): jnp.einsum('vpaj,pij->vai', inner.astype(jnp.bfloat16), b_occ, preferred_...  12.2 us
    dot_general x1, matrix products, products(): jnp.einsum('paj,vaj->vp', b_mixed, chosen, preferred_element_type=jnp.flo...  7.34 us
    dot_general x1, matrix products, products(): jnp.einsum('vp,paj->vaj', fit, b_mixed.astype(jnp.float32), precision=lax...  7.16 us
  transfers between devices with their start and end apart: 1, of which 1 were waited for; matrix products, arithmetic and copies ran while one was open for 6% of the time, Pallas kernels for 0%

commit v1 on v0

v1 whole, which is shorter than its diff:
```python
import jax
import jax.numpy as jnp
from jax import lax
from jax.sharding import PartitionSpec as P


def products(chosen, b_occ, b_vir, b_mixed, e_occ, e_vir):
    partial_value = jnp.einsum("paj,aj->p", b_mixed, chosen, preferred_element_type=jnp.float32)
    every_row = lax.all_gather(chosen, "aux", axis=0, tiled=True)
    inner = jnp.einsum("pab,bj->paj", b_vir, every_row, preferred_element_type=jnp.float32)
    fit = lax.psum(partial_value, "aux")
    exch = jnp.einsum(
        "paj,pij->ai", inner.astype(jnp.bfloat16), b_occ, preferred_element_type=jnp.float32
    )
    coul = jnp.sum(fit[:, None, None] * b_mixed.astype(jnp.float32), axis=0)
    gaps = e_vir[:, None] - e_occ[None, :]
    return gaps * chosen.astype(jnp.float32) + 2.0 * coul - exch


def local(trial, b_occ, b_vir, b_mixed, e_occ, e_vir, active):
    core = lax.axis_index("vec")
    first = active[0]
    other = lax.ppermute(trial[0], "vec", [(1, 0)])
    lead = jnp.where(first == 0, trial[0], jnp.where(first == 1, trial[1], other))
    chosen = jnp.where(core == 0, lead, trial[1])
    values = products(chosen, b_occ, b_vir, b_mixed, e_occ, e_vir).astype(jnp.bfloat16)
    back = lax.ppermute(values, "vec", [(0, 1)])
    zero = jnp.zeros_like(values)
    slot0 = jnp.where(
        core == 0, jnp.where(first == 0, values, zero), jnp.where(first == 2, back, zero)
    )
    slot1 = jnp.where((core == 1) | (first == 1), values, zero)
    return jnp.stack([slot0, slot1])


def solution(mesh):
    in_specs = (
        P(("grp", "vec"), "aux", None),
        P("grp", None, None),
        P("grp", "aux", None),
        P("grp", "aux", None),
        P("grp"),
        P(("grp", "aux")),
        P("grp"),
    )
    out_specs = P(("grp", "vec"), "aux", None)
    return jax.shard_map(local, mesh=mesh, in_specs=in_specs, out_specs=out_specs, check_vma=False)
```

time: 256 us -> 176 us (0.69)
  waiting for transfers between devices: 137 us -> 67.7 us
  matrix products: 80.2 us -> 58.2 us
  other arithmetic: 1.49 us -> 7.31 us
  starting transfers between devices: 0.01 us -> 2.63 us
    all_gather x1, waiting for transfers between devices: 136 us -> 64.4 us  [products(): every_row = lax.all_gather(chosen, 'aux', axis=0, tiled=True)]
    dot_general x4 -> x2, matrix products: 80.2 us -> 58.2 us  [the longest x1 50.8 us: products(): jnp.einsum('paj,pij->ai', inner.astype(jnp.bfloat16), b_occ, preferred_el...]
    reduce_sum x0 -> x1, other arithmetic: none -> 3.48 us  [products(): coul = jnp.sum(fit[:, None, None] * b_mixed.astype(jnp.float32), axis=0)]
    ppermute x0 -> x2, waiting for transfers between devices: none -> 3.29 us  [the longest x1 1.75 us: local(): back = lax.ppermute(values, 'vec', [(0, 1)])]
    ppermute x0 -> x2, starting transfers between devices: none -> 2.63 us  [the longest x1 1.34 us: local(): back = lax.ppermute(values, 'vec', [(0, 1)])]
  transfers between devices with their start and end apart: 1 -> 3, of which waited for: 1 -> 3; matrix products, arithmetic and copies ran while one was open for 6% -> 6% of each run, Pallas kernels for 0% -> 0%
where the time goes in v1:
time: 176 us
  waiting for transfers between devices  67.7 us (38%)
  matrix products  58.2 us (33%)
  blocking collectives  24 us (14%)
  between operations  14.8 us (8%)
  other arithmetic  7.31 us (4%)
  starting transfers between devices  2.63 us (1%)
    all_gather x1, waiting for transfers between devices, products(): every_row = lax.all_gather(chosen, 'aux', axis=0, tiled=True)  64.4 us
    dot_general x1, matrix products, products(): jnp.einsum('paj,pij->ai', inner.astype(jnp.bfloat16), b_occ, preferred_el...  50.8 us
    psum x1, blocking collectives, products(): fit = lax.psum(partial_value, 'aux')  24 us
    dot_general x1, matrix products, products(): jnp.einsum('paj,aj->p', b_mixed, chosen, preferred_element_type=jnp.float32)  7.43 us
  transfers between devices with their start and end apart: 3, of which 3 were waited for; matrix products, arithmetic and copies ran while one was open for 6% of the time, Pallas kernels for 0%

profile of v1, /device:TPU:0, one launch (start us, length us, event | category | flops | bytes accessed | tf_op | source)
XLA Modules:
  0.0 175.9 jit_solution(10504397194174432222)
XLA Ops:
  6.5 0.0 all-gather.2.cloned.1.call-start
  6.5 1.2 slice_bitcast_fusion
  7.7 1.3 collective-permute-start
  10.3 1.5 collective-permute-done
  11.9 2.3 %bitcast_select_fusion = bf16[592,640]{1,0:T(8,128)(2,1)} fusion(bf16[592,640]{1,0:T(8,128)(2,1)S(1)} %collective-permute-done, bf16[2,592,640]{2,1,0:T(8,128)(2,1)} %param.7, pred[]{:T(512)} %bitcast.2, pred[]{:T(512)} %bitcast, pred[]{:T(512)S(6)} %eq.27), kind=kLoop, calls=%fused_computation.13 | loop fusion | flops 1136640 | bytes 3031043 | tf_op jit(solution)/shard_map/jit(_where)/select_n | solution.py:25
  14.2 0.0 all-gather.2.cloned.1.call-update
  14.2 7.4 %fusion.11 = f32[6]{0:T(128)S(1)} fusion(bf16[6,592,640]{2,1,0:T(8,128)(2,1)} %param.10, bf16[592,640,1]{1,0,2:T(8,128)(2,1)} %bitcast.44), kind=kOutput, calls=%fused_computation.12 | convolution fusion | flops 4546560 | bytes 5304344 | tf_op jit(solution)/shard_map/paj,aj->p/dot_general | solution.py:8
  21.7 0.0 copy-start
  21.7 0.0 copy-start.1
  21.7 0.0 copy-start.2
  21.7 24.0 %psum.7 = f32[6]{0:T(128)S(1)} all-reduce(f32[6]{0:T(128)S(1)} %fusion.11), channel_id=1, replica_groups=mesh['grp'=2,'aux'=8,'vec'=2] {'aux'}, use_global_device_ids=true, to_apply=%region_0.1 | all-reduce | flops 6 | bytes 48 | tf_op jit(solution)/shard_map/psum | solution.py:11
  45.7 3.5 %multiply_reduce_fusion = f32[592,640]{1,0:T(8,128)S(1)} fusion(bf16[6,592,640]{2,1,0:T(8,128)(2,1)} %param.10, f32[6]{0:T(128)S(1)} %psum.7), kind=kLoop, calls=%fused_computation | loop fusion | flops 6440960 | bytes 6062104 | tf_op jit(solution)/shard_map/reduce_sum | solution.py:15
  49.2 0.0 copy-start.3
  49.2 64.4 %all-gather.2.cloned.1.call-done = bf16[4736,640]{1,0:T(8,128)(2,1)} async-done(((bf16[592,640]{1,0:T(8,128)(2,1)}), bf16[4736,640]{1,0:T(8,128)(2,1)}) %all-gather.2.cloned.1.call-update) | async-done | bytes 6062096 | tf_op jit(solution)/shard_map/all_gather | solution.py:9
  113.6 0.0 copy-done
  113.6 0.0 copy-done.1
  113.7 0.0 copy-done.2
  113.7 50.8 %fusion.7 = bf16[592,640]{1,0:T(8,128)(2,1)S(1)} fusion(f32[592,640]{1,0:T(8,128)S(1)} %multiply_reduce_fusion, bf16[592,640]{1,0:T(8,128)(2,1)S(1)} %copy-done, bf16[6,640,640]{2,1,0:T(8,128)(2,1)} %param.8, f32[640]{0:T(1024)S(1)} %copy-done.1, f32[592]{0:T(1024)S(1)} %copy-done.2, bf16[6,592,4736]{2,1,0:T(8,128)(2,1)} %param.9, ...), kind=kOutput, calls=%fused_computation.10 | convolution fusion | flops 24444958720 | bytes 47657792 | tf_op jit(solution)/shard_map/paj,pij->ai/dot_general | solution.py:12
  164.4 1.3 collective-permute-start.1
  165.8 0.0 copy-done.3
  165.8 1.8 collective-permute-done.1
  167.6 0.2 select_bitcast_fusion.1
  167.8 1.3 pad_maximum_fusion
Async XLA Ops:
  6.5 107.1 %all-gather.2.cloned.1.call-start = ((), (), s32[]{:S(2)}) async-start(), calls=%async_computation | async-start | bytes 6819840 | tf_op jit(solution)/shard_map/all_gather | solution.py:9
  7.7 4.1 %collective-permute-start = (bf16[592,640]{1,0:T(8,128)(2,1)S(1)}, bf16[592,640]{1,0:T(8,128)(2,1)S(1)}, u32[]{:S(2)}, u32[]{:S(2)}) collective-permute-start(bf16[592,640]{1,0:T(8,128)(2,1)S(1)} %slice_bitcast_fusion), channel_id=1, source_target_pairs={{1,0},{3,2},{5,4},{7,6},{9,8},{11,10},{13,12},{15,14},{17,16},{19,... | collective-permute-start | bytes 2273288 | tf_op jit(solution)/shard_map/ppermute | solution.py:23
  21.7 92.0 %copy-start = (bf16[592,640]{1,0:T(8,128)(2,1)S(1)}, bf16[592,640]{1,0:T(8,128)(2,1)}, u32[]{:S(2)}) copy-start(bf16[592,640]{1,0:T(8,128)(2,1)} %bitcast_select_fusion) | copy-start | bytes 2273284
  21.7 92.0 %copy-start.1 = (f32[640]{0:T(1024)S(1)}, f32[640]{0:T(1024)}, u32[]{:S(2)}) copy-start(f32[640]{0:T(1024)} %param.11) | copy-start | bytes 7684
  21.7 92.0 %copy-start.2 = (f32[592]{0:T(1024)S(1)}, f32[592]{0:T(1024)}, u32[]{:S(2)}) copy-start(f32[592]{0:T(1024)} %param.12) | copy-start | bytes 7108
  49.2 116.6 %copy-start.3 = (s32[2]{0:T(128)S(1)}, s32[2]{0:T(128)}, u32[]{:S(2)}) copy-start(s32[2]{0:T(128)} %param.13) | copy-start | bytes 28
  164.4 3.2 %collective-permute-start.1 = (bf16[592,640]{1,0:T(8,128)(2,1)S(1)}, bf16[592,640]{1,0:T(8,128)(2,1)S(1)}, u32[]{:S(2)}, u32[]{:S(2)}) collective-permute-start(bf16[592,640]{1,0:T(8,128)(2,1)S(1)} %fusion.7), channel_id=1, source_target_pairs={{0,1},{2,3},{4,5},{6,7},{8,9},{10,11},{12,13},{14,15},{16,17},{18,... | collective-permute-start | bytes 2273288 | tf_op jit(solution)/shard_map/ppermute | solution.py:27
Sparse Core Ops, SparseCore 0:
  14.4 99.2 all-gather.1

commit v2 on v1

v2 whole, which is shorter than its diff:
```python
import functools

import jax
import jax.numpy as jnp
from jax import lax
from jax.experimental import pallas as pl
from jax.experimental.pallas import tpu as pltpu
from jax.sharding import PartitionSpec as P

F32 = jnp.float32
BF16 = jnp.bfloat16
LANE = 128
STEP = 16
ZS, XS = 4, 2
ZX_CHUNKS = 5
SLOTS = 4
VISITS = (8, 10, 8, 4, 7)
LAST = VISITS[3] + VISITS[4]


def visit_starts(z, x):
    def pick(a, b, c, d):
        return jnp.where(z == 0, a, jnp.where(z == 1, b, jnp.where(z == 2, c, d)))

    first = pick(0, 10, 19, 29)
    second = pick(8, 0, 27, 19)
    third = pick(18, 18, 11, 11)
    low = pick(26, 26, 0, 0)
    early = low + jnp.where(x == 0, 0, VISITS[4])
    late = low + jnp.where(x == 0, VISITS[3], 0)
    return first, second, third, early, late


def visit_pairs(z):
    def pick(a, b, c, d):
        return jnp.where(z == 0, a, jnp.where(z == 1, b, jnp.where(z == 2, c, d)))

    return z, pick(1, 0, 3, 2), pick(2, 2, 1, 1), pick(3, 3, 0, 0)


def kernel(
    active, trial, b_occ, b_vir, b_mixed, e_occ, e_vir,
    mine, theirs,
    full, acc, occ, mixed, base, cand, vir, fits,
    load_sem, vir_sem, swap_send, swap_recv, back_send, back_recv, recv_sem, send_sem,
):
    aux = mixed.shape[0]
    rows, cols = mine.shape
    core = lax.axis_index("vec")
    at = lax.axis_index("aux")
    z, x = at // XS, at % XS
    step = 96
    tail = rows - ZX_CHUNKS * step
    XZ, FIT = ZX_CHUNKS, ZX_CHUNKS + 1

    loads = [
        pltpu.make_async_copy(trial.at[0], cand.at[0], load_sem.at[0]),
        pltpu.make_async_copy(trial.at[1], cand.at[1], load_sem.at[1]),
    ]
    load_mixed = pltpu.make_async_copy(b_mixed, mixed, load_sem.at[2])
    load_occ = pltpu.make_async_copy(b_occ, occ, load_sem.at[3])
    for load in loads:
        load.start()
    load_mixed.start()

    barrier = pltpu.get_barrier_semaphore()

    def greet(**where):
        pl.semaphore_signal(barrier, inc=1, device_id=where, device_id_type=pl.DeviceIdType.MESH)

    greet(vec=1 - core)
    greet(aux=z * XS + 1 - x)

    @pl.when(z < ZS - 1)
    def _():
        greet(aux=at + XS)

    @pl.when(z > 0)
    def _():
        greet(aux=at - XS)

    pl.semaphore_wait(barrier, 3 + jnp.where((z > 0) & (z < ZS - 1), 1, 0))

    swap = pltpu.make_async_remote_copy(
        src_ref=trial.at[0], dst_ref=cand.at[2], send_sem=swap_send, recv_sem=swap_recv,
        device_id={"vec": 1 - core}, device_id_type=pl.DeviceIdType.MESH,
    )

    @pl.when(core == 1)
    def _():
        swap.start()

    for load in loads:
        load.wait()

    @pl.when(core == 0)
    def _():
        swap.wait_recv()

    first = active[0]
    own = at * rows

    @pl.when(core == 1)
    def _():
        @pl.loop(0, rows // STEP)
        def _(r):
            here = pl.ds(pl.multiple_of(r * STEP, STEP), STEP)
            full[pl.ds(pl.multiple_of(own + r * STEP, STEP), STEP), :] = cand[1, here, :]

    @pl.when(core == 0)
    def _():
        @pl.loop(0, rows // STEP)
        def _(r):
            here = pl.ds(pl.multiple_of(r * STEP, STEP), STEP)
            a, b, c = cand[0, here, :], cand[1, here, :], cand[2, here, :]
            full[pl.ds(pl.multiple_of(own + r * STEP, STEP), STEP), :] = jnp.where(
                first == 0, a, jnp.where(first == 1, b, c)
            )

    def piece(block, m, kind):
        if kind == "fit":
            return fits.at[block]
        if kind == "xz":
            return full.at[pl.ds(pl.multiple_of(block * rows + ZX_CHUNKS * step, STEP), tail), :]
        return full.at[pl.ds(pl.multiple_of(block * rows + m * step, STEP), step), :]

    def index(m, kind):
        return FIT if kind == "fit" else XZ if kind == "xz" else m

    def copy(block, m, kind, way):
        target = (z * XS + 1 - x, at + XS, at - XS)[way]
        part, i = piece(block, m, kind), index(m, kind)
        return pltpu.make_async_remote_copy(
            src_ref=part, dst_ref=part,
            send_sem=send_sem.at[way, block, i], recv_sem=recv_sem.at[block, i],
            device_id={"aux": target}, device_id_type=pl.DeviceIdType.MESH,
        )

    def arrived(block, m, kind):
        copy(block, m, kind, 0).wait_recv()

    def pass_on(s, y_own, m, kind, act):
        block = s * XS + (x if y_own else 1 - x)
        if y_own:
            if kind == "xz":
                @pl.when(z == s)
                def _():
                    act(copy(block, m, kind, 0))
            else:
                act(copy(block, m, kind, 0))
        if y_own or kind == "xz":
            @pl.when((z >= s) & (z < ZS - 1))
            def _():
                act(copy(block, m, kind, 1))

            @pl.when((z <= s) & (z > 0))
            def _():
                act(copy(block, m, kind, 2))

    def start(c):
        c.start()

    def forward(d, m, kind):
        for s, there in ((z - d, z >= d), (z + d, z + d < ZS)):
            @pl.when(there)
            def _():
                arrived(s * XS + x, m, kind)
                pass_on(s, True, m, kind, start)
                if kind == "xz":
                    arrived(s * XS + 1 - x, m, kind)
                    pass_on(s, False, m, kind, start)

    def partner_chunks(s):
        @pl.loop(0, ZX_CHUNKS)
        def _(m):
            arrived(s * XS + 1 - x, m, "zx")

    pass_on(z, True, 0, "xz", start)

    @pl.loop(0, ZX_CHUNKS)
    def _(m):
        pass_on(z, True, m, "zx", start)

    starts = visit_starts(z, x)

    def fetch(v, p):
        width = VISITS[v] * LANE
        slot = (v * aux + p) % SLOTS
        return pltpu.make_async_copy(
            b_vir.at[p, :, pl.ds(pl.multiple_of(starts[v] * LANE, LANE), width)],
            vir.at[slot, :, pl.ds(0, width)],
            vir_sem.at[slot],
        )

    for p in range(SLOTS - 1):
        fetch(0, p).start()
    load_occ.start()

    load_mixed.wait()

    def fit_step(r, sums):
        here = pl.ds(pl.multiple_of(r * STEP, STEP), STEP)
        t = full[pl.ds(pl.multiple_of(own + r * STEP, STEP), STEP), :].astype(F32)
        new = []
        for p in range(aux):
            prod = mixed[p, here, :].astype(F32) * t
            prod = prod[:8] + prod[8:]
            new.append(
                sums[p] + sum(prod[:, k * LANE:(k + 1) * LANE] for k in range(cols // LANE))
            )
        return tuple(new)

    sums = lax.fori_loop(
        0, rows // STEP, fit_step, tuple(jnp.zeros((8, LANE), F32) for _ in range(aux))
    )
    for p in range(aux):
        fits[at, pl.ds(p, 1), :] = jnp.broadcast_to(jnp.sum(sums[p]).reshape(1, 1), (1, LANE))
    pass_on(z, True, 0, "fit", start)

    arrived(z * XS + 1 - x, 0, "xz")
    pass_on(z, False, 0, "xz", start)

    @pl.loop(0, ZX_CHUNKS)
    def _(m):
        forward(1, m, "zx")

    forward(1, 0, "xz")
    forward(1, 0, "fit")

    def visit(v, d):
        width = VISITS[v] * LANE
        begin = pl.multiple_of(starts[v] * LANE, LANE)

        @pl.loop(0, aux)
        def _(p):
            fetch(v, p).wait()

            @pl.when(p + SLOTS - 1 < aux)
            def _():
                fetch(v, p + SLOTS - 1).start()

            if v + 1 < len(VISITS):
                @pl.when(p + SLOTS - 1 >= aux)
                def _():
                    fetch(v + 1, p + SLOTS - 1 - aux).start()

            if d:
                @pl.when(p < ZX_CHUNKS)
                def _():
                    forward(d, p, "zx")

            part = jnp.dot(
                vir[(v * aux + p) % SLOTS, :, :width], full[pl.ds(begin, width), :],
                preferred_element_type=F32,
            )
            if v == 0:
                acc[p] = part
            else:
                acc[p] += part

        if d:
            forward(d, 0, "xz")
            forward(d, 0, "fit")

    pairs = visit_pairs(z)
    partner_chunks(pairs[0])
    visit(0, 2)
    partner_chunks(pairs[1])
    visit(1, 3)
    partner_chunks(pairs[2])
    visit(2, 0)

    for s in range(ZS):
        arrived(s * XS + 1 - x, 0, "fit")
    fit = fits[0]
    for b in range(1, ZS * XS):
        fit = fit + fits[b]

    @pl.loop(0, rows // STEP)
    def _(r):
        here = pl.ds(pl.multiple_of(r * STEP, STEP), STEP)
        t = full[pl.ds(pl.multiple_of(own + r * STEP, STEP), STEP), :].astype(F32)
        coul = fit[0:1, 0:1] * mixed[0, here, :].astype(F32)
        for p in range(1, aux):
            coul += fit[p:p + 1, 0:1] * mixed[p, here, :].astype(F32)
        base[here, :] = (e_vir[here, :] - e_occ[...]) * t + 2.0 * coul

    visit(3, 0)
    partner_chunks(pairs[3])
    visit(4, 0)

    load_occ.wait()
    half = (rows // 2 + STEP - 1) // STEP * STEP

    def back(k):
        here = pl.ds(0, half) if k == 0 else pl.ds(half, rows - half)
        return pltpu.make_async_remote_copy(
            src_ref=mine.at[here, :], dst_ref=theirs.at[here, :],
            send_sem=back_send.at[k], recv_sem=back_recv.at[k],
            device_id={"vec": 1 - core}, device_id_type=pl.DeviceIdType.MESH,
        )

    for k, here in enumerate((slice(0, half), slice(half, rows))):
        @pl.loop(0, aux)
        def _(p):
            base[here, :] -= lax.dot_general(
                acc[p, here, :].astype(BF16), occ[p], (((1,), (1,)), ((), ())),
                preferred_element_type=F32,
            )

        mine[here, :] = base[here, :].astype(BF16)

        @pl.when(core == 0)
        def _():
            back(k).start()

    def sent(c):
        c.wait_send()

    for s in range(ZS):
        @pl.loop(0, ZX_CHUNKS)
        def _(m):
            pass_on(s, True, m, "zx", sent)

        pass_on(s, True, 0, "xz", sent)
        pass_on(s, False, 0, "xz", sent)
        pass_on(s, True, 0, "fit", sent)

    @pl.when(core == 1)
    def _():
        swap.wait_send()
        for k in range(2):
            back(k).wait_recv()

    @pl.when(core == 0)
    def _():
        for k in range(2):
            back(k).wait_send()


def fused(trial, b_occ, b_vir, b_mixed, e_occ, e_vir, active):
    _, rows, cols = trial.shape
    aux, _, total = b_vir.shape
    blocks = ZS * XS
    widest = max(VISITS) * LANE
    hbm = pl.BlockSpec(memory_space=pl.ANY)
    vmem = pl.BlockSpec(memory_space=pltpu.VMEM)
    dma = pltpu.SemaphoreType.DMA
    block = jax.ShapeDtypeStruct((rows, cols), BF16)
    flops = 2 * aux * rows * cols * (total + cols)
    return pl.pallas_call(
        kernel,
        out_shape=(block, block),
        in_specs=[pl.BlockSpec(memory_space=pltpu.SMEM), hbm, hbm, hbm, hbm, vmem, vmem],
        out_specs=(vmem, vmem),
        scratch_shapes=[
            pltpu.VMEM((total, cols), BF16),
            pltpu.VMEM((aux, rows, cols), F32),
            pltpu.VMEM((aux, cols, cols), BF16),
            pltpu.VMEM((aux, rows, cols), BF16),
            pltpu.VMEM((rows, cols), F32),
            pltpu.VMEM((3, rows, cols), BF16),
            pltpu.VMEM((SLOTS, rows, widest), BF16),
            pltpu.VMEM((blocks, 8, LANE), F32),
            dma((4,)), dma((SLOTS,)), dma, dma, dma((2,)), dma((2,)),
            dma((blocks, ZX_CHUNKS + 2)), dma((3, blocks, ZX_CHUNKS + 2)),
        ],
        compiler_params=pltpu.CompilerParams(
            collective_id=0, has_side_effects=True, vmem_limit_bytes=56 * 2**20
        ),
        cost_estimate=pl.CostEstimate(
            flops=flops, bytes_accessed=2 * aux * rows * total, transcendentals=0
        ),
    )(active, trial, b_occ, b_vir, b_mixed, e_occ[None, :], e_vir[:, None])


def plain(trial, b_occ, b_vir, b_mixed, e_occ, e_vir, active):
    core = lax.axis_index("vec")
    first = active[0]
    other = lax.ppermute(trial[0], "vec", [(1, 0)])
    lead = jnp.where(first == 0, trial[0], jnp.where(first == 1, trial[1], other))
    chosen = jnp.where(core == 0, lead, trial[1])
    part = jnp.einsum("paj,aj->p", b_mixed, chosen, preferred_element_type=F32)
    every_row = lax.all_gather(chosen, "aux", axis=0, tiled=True)
    inner = jnp.einsum("pab,bj->paj", b_vir, every_row, preferred_element_type=F32)
    fit = lax.psum(part, "aux")
    exch = jnp.einsum("paj,pij->ai", inner.astype(BF16), b_occ, preferred_element_type=F32)
    coul = jnp.sum(fit[:, None, None] * b_mixed.astype(F32), axis=0)
    gaps = e_vir[:, None] - e_occ[None, :]
    values = (gaps * chosen.astype(F32) + 2.0 * coul - exch).astype(BF16)
    return values, lax.ppermute(values, "vec", [(0, 1)])


def local(small, trial, b_occ, b_vir, b_mixed, e_occ, e_vir, active):
    core = lax.axis_index("vec")
    first = active[0]
    work = fused if small and trial.shape[1] == 592 and trial.shape[2] == 640 else plain
    values, back = work(trial, b_occ, b_vir, b_mixed, e_occ, e_vir, active)
    zero = jnp.zeros_like(values)
    slot0 = jnp.where(
        core == 0, jnp.where(first == 0, values, zero), jnp.where(first == 2, back, zero)
    )
    slot1 = jnp.where((core == 1) | (first == 1), values, zero)
    return jnp.stack([slot0, slot1])


def solution(mesh):
    in_specs = (
        P(("grp", "vec"), "aux", None),
        P("grp", None, None),
        P("grp", "aux", None),
        P("grp", "aux", None),
        P("grp"),
        P(("grp", "aux")),
        P("grp"),
    )
    out_specs = P(("grp", "vec"), "aux", None)
    run = functools.partial(local, mesh.shape["aux"] == ZS * XS)
    return jax.shard_map(run, mesh=mesh, in_specs=in_specs, out_specs=out_specs, check_vma=False)
```

time: 176 us -> 104 us (0.59)
  Pallas kernels: 0 us -> 95.9 us
  waiting for transfers between devices: 67.7 us -> 0 us
  matrix products: 58.2 us -> 0 us
  blocking collectives: 24 us -> 0 us
  between operations: 14.8 us -> 1.96 us
  other arithmetic: 7.31 us -> 2.6 us
  starting transfers between devices: 2.63 us -> 0 us
    pallas_call x0 -> x1, Pallas kernels: none -> 95.9 us  [fused(): pl.pallas_call(kernel, out_shape=(block, block), in_specs=[pl.BlockSpec(m...]
    all_gather x1 -> x0, waiting for transfers between devices: 64.4 us -> none  [products(): every_row = lax.all_gather(chosen, 'aux', axis=0, tiled=True)]
    dot_general x2 -> x0, matrix products: 58.2 us -> none  [the longest x1 50.8 us: products(): jnp.einsum('paj,pij->ai', inner.astype(jnp.bfloat16), b_occ, preferred_el...]
    psum x1 -> x0, blocking collectives: 24 us -> none  [products(): fit = lax.psum(partial_value, 'aux')]
    reduce_sum x1 -> x0, other arithmetic: 3.48 us -> none  [products(): coul = jnp.sum(fit[:, None, None] * b_mixed.astype(jnp.float32), axis=0)]
    ppermute x2 -> x0, waiting for transfers between devices: 3.29 us -> none  [the longest x1 1.75 us: local(): back = lax.ppermute(values, 'vec', [(0, 1)])]
    broadcast_in_dim x0 -> x2, local copies, waits for them, and re-layouts: none -> 2.81 us  [the longest x1 1.55 us: fused(): e_vir[:, None]]
    ppermute x2 -> x0, starting transfers between devices: 2.63 us -> none  [the longest x1 1.34 us: local(): back = lax.ppermute(values, 'vec', [(0, 1)])]
  transfers between devices with their start and end apart: 3 -> 0, of which waited for: 3 -> 0; matrix products, arithmetic and copies ran while one was open for 6% -> 0% of each run, Pallas kernels for 0% -> 0%
where the time goes in v2:
time: 104 us; the launch traced here: 103 us
  Pallas kernels  95.9 us (92%)
  local copies, waits for them, and re-layouts  2.81 us (3%)
  other arithmetic  2.6 us (2%)
  between operations  1.96 us (2%)
    pallas_call x1, Pallas kernels, fused(): pl.pallas_call(kernel, out_shape=(block, block), in_specs=[pl.BlockSpec(m...  95.9 us
    another operation x2, other arithmetic, local(): return jnp.stack([slot0, slot1])  2.6 us

profile of v2, /device:TPU:0, one launch (start us, length us, event | category | flops | bytes accessed | tf_op | source)
XLA Modules:
  0.0 103.3 jit_solution(14728906328794980704)
XLA Ops:
  1.9 1.3 %broadcast_in_dim.9.e_occ = f32[1,640]{1,0:T(1,128)} reshape(f32[640]{0:T(1024)} %param.11) | data formatting | bytes 5120 | tf_op jit(solution)/shard_map/broadcast_in_dim | solution.py:374
  3.2 1.5 %broadcast_in_dim.12.e_vir = f32[592,1]{1,0:T(8,128)} reshape(f32[592]{0:T(1024)} %param.12) | data formatting | bytes 4736 | tf_op jit(solution)/shard_map/broadcast_in_dim | solution.py:374
  4.8 95.9 %shard_map.73 = (bf16[592,640]{1,0:T(8,128)(2,1)}, bf16[592,640]{1,0:T(8,128)(2,1)}) custom-call(s32[2]{0:T(128)} %active.1, bf16[2,592,640]{2,1,0:T(8,128)(2,1)} %trial.1, bf16[6,640,640]{2,1,0:T(8,128)(2,1)} %b_occ.1, bf16[6,592,4736]{2,1,0:T(8,128)(2,1)} %b_vir.1, bf16[6,592,640]{2,1,0:T(8,128)(2,1)} %b_mixed.1, f32[1,640]{1,0:T(1,128)} %broadcast_in_dim.9.e_occ, ...), custom_call_target="tpu_custom_call" | custom-call | flops 24442306560 | bytes 33644544 | tf_op jit(solution)/shard_map/pallas_call | solution.py:351
  100.7 1.3 %select_bitcast_fusion.1 = (bf16[1,592,640]{2,1,0:T(8,128)(2,1)S(1)}, bf16[1,592,640]{2,1,0:T(8,128)(2,1)S(1)}) fusion(bf16[592,640]{1,0:T(8,128)(2,1)} %get-tuple-element.8, bf16[592,640]{1,0:T(8,128)(2,1)} %get-tuple-element.7, pred[]{:T(512)} %bitcast.1, pred[]{:T(512)} %bitcast, pred[]{:T(512)S(6)} %eq.24, pred[]{:T(512)S(6)} %or.3), kind=kLoop, calls=%fused_computation.2 | loop fusion | flops 1515520 | bytes 3031044 | tf_op jit(solution)/shard_map/stack | solution.py:404
  102.0 1.3 %pad_maximum_fusion = bf16[2,592,640]{2,1,0:T(8,128)(2,1)} fusion(bf16[1,592,640]{2,1,0:T(8,128)(2,1)S(1)} %get-tuple-element.10, bf16[1,592,640]{2,1,0:T(8,128)(2,1)S(1)} %get-tuple-element.9), kind=kLoop, calls=%fused_computation | loop fusion | flops 757760 | bytes 3031040 | tf_op jit(solution)/shard_map/stack | solution.py:404
